TPU v7x, 32 devices: a whole 2x2x4 slice. The times are simulated.
32 devices in a mesh: rep: 4 (over z), fsdp: 8 (over y, x, core).
Axes of the slice: x: 2, y: 2, z: 4, core: 2. Of those that a mesh axis runs over, the one named last changes fastest.
Arguments:
- grads: bfloat16 [4, 1024, 16384], P('rep', 'fsdp')
- moments: float32 [1024, 16384], P('fsdp', 'rep'), may hold values from 0.05 to 2
- factors: float32 [4, 8, 1024, 1024], P('rep', 'fsdp'), as said below
- roots: bfloat16 [4, 8, 1024, 1024], P('rep', 'fsdp'), as said below
- refresh: int32 [8], replicated, may hold values from 0 to 31, as said below
- owner: int32 [1, 16], replicated, may hold values from 0 to 3, as said below
Outputs:
- update: bfloat16 [1024, 16384], P('fsdp')
- new_moments: float32 [1024, 16384], P('fsdp', 'rep')
- new_factors: float32 [4, 8, 1024, 1024], P('rep', 'fsdp')
- new_roots: bfloat16 [4, 8, 1024, 1024], P('rep', 'fsdp')
Inputs may be any that keep to these rules, and one draw needn't show every extreme that they name: `refresh`: 8 distinct factor ids below 32; no two of them are held at the same fsdp index. `owner`: every band gives exactly 4 of its column blocks to each group. `factors`: each matrix is symmetric and positive definite. `roots`: each matrix is symmetric.
All inputs are finite; a program needn't handle non-finite values.
Results may differ from a plain program's by a relative error of at most 0.015.
Values may be sent and summed in bfloat16 or wider, within the bound.
A program may use at most 128 MiB of HBM per device.

v0:
```python
import jax
import jax.numpy as jnp
from jax import lax
from jax.sharding import PartitionSpec as P

NEWTON = 3


BETA_FACTOR = 0.9
BETA_MOMENT = 0.95
EPS_ADAM = 1e-08
EPS_NORM = 1e-06


def from_partner(shard, axis, stride):
    return lax.ppermute(shard, axis, [(i, i ^ 1 << stride) for i in range(lax.axis_size(axis))])


def newton_seed(factor):
    norm_value = jnp.sqrt(jnp.sum(factor * factor))
    state_now = (factor / norm_value).astype(jnp.bfloat16)
    first_scale = norm_value ** (-0.25)
    return (state_now, first_scale)


def newton_step_matrix(state_now, identity):
    return ((5.0 * identity - state_now.astype(jnp.float32)) * 0.25).astype(jnp.bfloat16)


def newton_whole(factor):
    identity = jnp.eye(factor.shape[0], dtype=jnp.float32)
    state_now, first_scale = newton_seed(factor)
    root_now = (first_scale * identity).astype(jnp.bfloat16)
    for iteration in range(NEWTON):
        step_mat = newton_step_matrix(state_now, identity)
        root_now = jnp.dot(root_now, step_mat, preferred_element_type=jnp.float32).astype(
            jnp.bfloat16
        )
        if iteration + 1 < NEWTON:
            square = jnp.dot(step_mat, step_mat, preferred_element_type=jnp.float32).astype(
                jnp.bfloat16
            )
            fourth = jnp.dot(square, square, preferred_element_type=jnp.float32).astype(
                jnp.bfloat16
            )
            state_now = jnp.dot(fourth, state_now, preferred_element_type=jnp.float32).astype(
                jnp.bfloat16
            )
    return root_now


def local(grads, moments, factors, roots, refresh, owner):
    block_size = factors.shape[2]
    height = grads.shape[1]
    width_all = grads.shape[2]
    band_span = block_size // height
    groups = lax.axis_size("rep")
    columns = width_all // block_size
    per_group = columns // groups
    fsdp_count = lax.axis_size("fsdp")
    sub_rows = block_size // fsdp_count
    band_count = height // sub_rows
    half_cols = block_size // 2
    group_index = lax.axis_index("rep")
    fsdp_index = lax.axis_index("fsdp")
    band_index = fsdp_index // band_span
    local_index = fsdp_index % band_span
    side_index = local_index % 2
    slot_index = local_index // 2
    col_range = jnp.arange(columns, dtype=jnp.int32)
    col_order = jnp.argsort(owner * columns + col_range[None, :], axis=1)
    replica_term = grads[0].astype(jnp.float32)
    summed = lax.psum(replica_term.astype(jnp.bfloat16), "rep").astype(jnp.float32)
    mine_cols = lax.dynamic_slice_in_dim(col_order, group_index * per_group, per_group, 1)
    owned_grad = jnp.take_along_axis(
        summed.reshape(band_count, sub_rows, columns, block_size),
        mine_cols[:, None, :, None],
        axis=2,
    )
    gradient = owned_grad / groups
    moment_old = moments.reshape(band_count, sub_rows, per_group, block_size)
    moment_new = BETA_MOMENT * moment_old + (1.0 - BETA_MOMENT) * gradient * gradient
    adam_dir = gradient / (jnp.sqrt(moment_new) + EPS_ADAM)
    adam_table = jnp.sum(adam_dir * adam_dir, axis=(1, 3))
    pieces = jnp.transpose(gradient.astype(jnp.bfloat16), (0, 2, 1, 3)).reshape(
        band_count * per_group, sub_rows, block_size
    )
    outgoing = jnp.repeat(pieces, 2, axis=0)
    incoming = lax.all_to_all(outgoing, "fsdp", split_axis=0, concat_axis=0, tiled=True)
    whole_block = incoming.reshape(block_size, block_size)
    operand = jnp.where(side_index == 0, whole_block, whole_block.T)
    gram_matrix = lax.dot_general(
        operand, operand, (((1,), (1,)), ((), ())), preferred_element_type=jnp.float32
    )
    new_factor = BETA_FACTOR * factors[0, 0] + (1.0 - BETA_FACTOR) * gram_matrix
    own_root = roots[0, 0]
    partner_root = from_partner(own_root, "fsdp", 0)
    left_root = jnp.where(side_index == 0, own_root, partner_root)
    right_root = jnp.where(side_index == 0, partner_root, own_root)
    right_cols = lax.dynamic_slice_in_dim(right_root, side_index * half_cols, half_cols, 1)
    mixed_rows = jnp.dot(left_root, whole_block, preferred_element_type=jnp.float32).astype(
        jnp.bfloat16
    )
    product = jnp.dot(mixed_rows, right_cols, preferred_element_type=jnp.float32)
    product_part = jnp.sum(product * product)
    band_mask = (jnp.arange(band_count) == band_index).astype(jnp.float32)[:, None]
    slot_mask = (jnp.arange(per_group) == slot_index).astype(jnp.float32)[None, :]
    product_table = band_mask * slot_mask * product_part
    adam_total, product_total = lax.psum((adam_table, product_table), "fsdp")
    adam_sq = jnp.sum(adam_total * band_mask * slot_mask)
    product_sq = jnp.sum(product_total * band_mask * slot_mask)
    graft_scale = jnp.sqrt(adam_sq) * lax.rsqrt(product_sq + EPS_NORM)
    update_half = (product * graft_scale).astype(jnp.bfloat16)
    outgoing_rows = update_half.reshape(fsdp_count, sub_rows, half_cols)
    incoming_rows = lax.all_to_all(outgoing_rows, "fsdp", split_axis=0, concat_axis=0, tiled=True)
    arranged_rows = incoming_rows.reshape(band_count, per_group, 2, sub_rows, half_cols)
    update_slab = jnp.transpose(arranged_rows, (0, 3, 1, 2, 4)).reshape(
        height, per_group * block_size
    )
    everything = lax.all_gather(update_slab, "rep", axis=1, tiled=True)
    inverse = jnp.argsort(col_order, axis=1)
    update = jnp.take_along_axis(
        everything.reshape(band_count, sub_rows, columns, block_size),
        inverse[:, None, :, None],
        axis=2,
    ).reshape(height, width_all)
    pair_ids = refresh // 2
    listed_band = pair_ids // columns
    listed_col = pair_ids % columns
    listed_rows = jnp.take(owner, listed_band, axis=0)
    listed_group = jnp.take_along_axis(listed_rows, listed_col[:, None], axis=1)[:, 0]
    listed_rank = jnp.sum(
        (
            (listed_rows == listed_group[:, None]) & (col_range[None, :] < listed_col[:, None])
        ).astype(jnp.int32),
        axis=1,
    )
    listed_fsdp = listed_band * band_span + 2 * listed_rank + refresh % 2
    chosen = jnp.any((listed_group == group_index) & (listed_fsdp == fsdp_index))
    new_root = lax.cond(chosen, newton_whole, lambda matrix: own_root, new_factor)
    new_moments = moment_new.reshape(height, per_group * block_size)
    return (update, new_moments, new_factor[None, None], new_root[None, None])


def solution(mesh):
    placed = (
        P("rep", "fsdp", None),
        P("fsdp", "rep"),
        P("rep", "fsdp", None, None),
        P("rep", "fsdp", None, None),
        P(),
        P(),
    )
    return jax.shard_map(
        local,
        mesh=mesh,
        in_specs=placed,
        out_specs=(
            P("fsdp", None),
            P("fsdp", "rep"),
            P("rep", "fsdp", None, None),
            P("rep", "fsdp", None, None),
        ),
        check_vma=False,
    )
```

profile of v0, /device:TPU:6, one launch (start us, length us, event | category | flops | bytes accessed | tf_op | source)
XLA Modules:
  0.0 392.3 jit_solution(1301568624783009447)
XLA Ops:
  7.2 3.1 copy.91
  10.3 6.4 %copy.72 = bf16[1,128,16384]{1,2,0:T(8,128)(2,1)} copy(bf16[1,128,16384]{2,1,0:T(8,128)(2,1)} %param.8) | data formatting | bytes 8388608 | tf_op args[0]
  16.6 6.4 %copy.73 = bf16[1,128,16,1024]{3,1,2,0:T(8,128)(2,1)} copy(bf16[1,128,16,1024]{1,3,2,0:T(8,128)(2,1)} %bitcast.85) | data formatting | bytes 8388608 | tf_op jit(solution)/shard_map/reshape | solution.py:76
  23.8 0.7 sort.31
  24.6 154.8 %all-reduce.3.cloned.1.call-done = bf16[1,128,16,1024]{3,1,2,0:T(8,128)(2,1)} async-done(((bf16[1,128,16,1024]{3,1,2,0:T(8,128)(2,1)}), bf16[1,128,16,1024]{3,1,2,0:T(8,128)(2,1)}) %all-reduce.3.cloned.1.call-update) | async-done | bytes 4194320 | tf_op jit(solution)/shard_map/psum | solution.py:73
  179.4 6.5 %bitcast_convert_fusion = f32[128,16,1024]{2,0,1:T(8,128)} fusion(bf16[1,128,16,1024]{3,1,2,0:T(8,128)(2,1)} %all-reduce.3.cloned.1.call-done), kind=kLoop, calls=%fused_computation.51 | loop fusion | flops 2097152 | bytes 12582912 | tf_op jit(solution)/shard_map/reshape | solution.py:76
  185.9 4.1 %gather_fusion = f32[4,128,1024]{2,1,0:T(8,128)S(1)} fusion(f32[128,16,1024]{2,0,1:T(8,128)} %bitcast_convert_fusion, s32[1024]{0:T(1024)S(1)} %pad_clamp_fusion.1), kind=kCustom, calls=%fused_computation | custom fusion | bytes 4194320 | tf_op jit(solution)/shard_map/jit(take_along_axis)/gather | solution.py:75
  190.0 1.3 fusion.89
  191.3 1.6 copy.74
  192.9 1.6 broadcast_in_dim.79
  194.5 4.8 %all-to-all-start = ((bf16[8,128,1024]{1,2,0:T(8,128)(2,1)}), bf16[8,128,1024]{1,2,0:T(8,128)(2,1)}, u32[]{:S(2)}, u32[]{:S(2)}) async-start(bf16[8,128,1024]{1,2,0:T(8,128)(2,1)} %bitcast.86), calls=%async_computation | async-start | bytes 4194304 | tf_op jit(solution)/shard_map/all_to_all | solution.py:89
  199.3 2.9 copy.77
  202.2 1.8 copy.76
  204.0 4.3 %multiply_add_fusion = (f32[128,4096]{0,1:T(8,128)}, f32[4096]{0:T(1024)S(1)}) fusion(f32[128,4096]{0,1:T(8,128)} %copy.77, f32[128,4,1024]{0,2,1:T(8,128)} %copy.76, pred[4096]{0:T(1024)(128)(4,1)S(1)} %bitcast.94), kind=kLoop, calls=%fused_computation.62 | loop fusion | flops 5238784 | bytes 6311936 | tf_op jit(solution)/shard_map/add | solution.py:82
  208.5 15.2 %all-to-all-done = bf16[8,128,1024]{1,2,0:T(8,128)(2,1)} async-done(((bf16[8,128,1024]{1,2,0:T(8,128)(2,1)}), bf16[8,128,1024]{1,2,0:T(8,128)(2,1)}, u32[]{:S(2)}, u32[]{:S(2)}) %all-to-all-start) | async-done | bytes 2097184 | tf_op jit(solution)/shard_map/all_to_all | solution.py:89
  223.6 2.9 copy.75
  226.5 7.5 %multiply_reduce_fusion.1 = (f32[]{:T(128)}, f32[1024,512]{1,0:T(8,128)}) fusion(bf16[1024,1024]{1,0:T(8,128)(2,1)} %bitcast.2, s32[]{:T(128)S(6)} %select_n.156, bf16[1024,1024]{1,0:T(8,128)(2,1)} %collective-permute-done, pred[]{:T(512)S(6)} %eq.62, bf16[1024,1024]{1,0:T(8,128)(2,1)S(1)} %bitcast.87), kind=kOutput, calls=%fused_computation.60 | convolution fusion | flops 3224895488 | bytes 10487300 | tf_op jit(solution)/shard_map/dot_general | solution.py:104
  234.7 11.2 %all-reduce = (f32[1,4]{1,0:T(1,128)S(1)}, f32[1,4]{1,0:T(1,128)S(1)}) all-reduce(f32[1,4]{1,0:T(1,128)S(1)} %bitcast.97, f32[1,4]{1,0:T(1,128)S(1)} %select_multiply_fusion), channel_id=1, replica_groups=mesh['rep'=4,'fsdp'=8] {'fsdp'}, use_global_device_ids=true, to_apply=%region_5.6 | all-reduce | flops 8 | bytes 64 | tf_op jit(solution)/shard_map/psum | solution.py:109
  248.0 1.9 multiply_convert_fusion
  249.9 18.7 %all_to_all.10 = bf16[8,128,512]{2,1,0:T(8,128)(2,1)S(1)} all-to-all(bf16[8,128,512]{2,1,0:T(8,128)(2,1)S(1)} %bitcast.92), channel_id=1, replica_groups=mesh['rep'=4,'fsdp'=8] {'fsdp'}, dimensions={0} | all-to-all | bytes 2097152 | tf_op jit(solution)/shard_map/all_to_all | solution.py:115
  268.6 1.4 copy.78
  272.3 0.7 sort.32
  273.2 2.9 copy.83
  276.1 2.5 copy.81
  278.6 6.3 %bitcast_add_fusion = f32[1024,1024]{1,0:T(8,128)S(1)} fusion(f32[1,1,1024,1024]{3,2,1,0:T(8,128)} %param.10, bf16[1024,1024]{1,0:T(8,128)(2,1)S(1)} %bitcast.89, bf16[1024,1024]{0,1:T(8,128)(2,1)} %copy.81, pred[]{:T(512)S(6)} %eq.62), kind=kOutput, calls=%fused_computation.52 | convolution fusion | flops 2151677952 | bytes 12582913 | tf_op jit(solution)/shard_map/dot_general | solution.py:92
  284.9 2.0 copy-done
  286.9 63.0 %all-gather.2.cloned.1.call-done = bf16[128,16384]{0,1:T(8,128)(2,1)} async-done(((bf16[128,4096]{0,1:T(8,128)(2,1)}), bf16[128,16384]{0,1:T(8,128)(2,1)}) %all-gather.2.cloned.1.call-update) | async-done | bytes 4194320 | tf_op jit(solution)/shard_map/all_gather | solution.py:120
  349.9 6.4 %copy.79 = bf16[128,16,1024]{2,0,1:T(8,128)(2,1)} copy(bf16[128,16,1024]{0,2,1:T(8,128)(2,1)} %bitcast.90) | data formatting | bytes 8388608 | tf_op jit(solution)/shard_map/reshape | solution.py:123
  356.3 4.9 %gather_fusion.1 = bf16[16,128,1024]{2,1,0:T(8,128)(2,1)} fusion(bf16[128,16,1024]{2,0,1:T(8,128)(2,1)} %copy.79, s32[1024]{0:T(1024)S(1)} %pad_clamp_fusion), kind=kCustom, calls=%fused_computation.1 | custom fusion | bytes 8388672 | tf_op jit(solution)/shard_map/jit(take_along_axis)/gather | solution.py:122
  361.2 6.4 %copy.80 = bf16[128,16,1024]{0,2,1:T(8,128)(2,1)} copy(bf16[128,16,1024]{2,0,1:T(8,128)(2,1)} %bitcast.84) | data formatting | bytes 8388608 | tf_op jit(solution)/shard_map/jit(take_along_axis)/gather | solution.py:122
  367.6 11.5 %bitcast_select_fusion = bf16[128,16384]{0,1:T(8,128)(2,1)} fusion(bf16[128,16,1024]{0,2,1:T(8,128)(2,1)} %copy.80, pred[16384]{0:T(1024)(128)(4,1)S(1)} %bitcast.93), kind=kLoop, calls=%fused_computation.53 | loop fusion | flops 2097152 | bytes 8404992 | tf_op jit(solution)/shard_map/jit(take_along_axis)/select_n | solution.py:122
  379.1 6.4 %copy.82 = bf16[128,16384]{1,0:T(8,128)(2,1)} copy(bf16[128,16384]{0,1:T(8,128)(2,1)} %bitcast_select_fusion) | data formatting | bytes 8388608
  (42 shorter events, 4.3 us)
Async XLA Ops:
  7.2 172.3 %all-reduce.3.cloned.1.call-start = ((), (), s32[]{:S(2)}) async-start(), calls=%async_computation.2 | async-start | bytes 8388608 | tf_op jit(solution)/shard_map/psum | solution.py:73
  23.0 0.7 copy-start.2
  23.1 203.4 %collective-permute-start = (bf16[1024,1024]{1,0:T(8,128)(2,1)}, bf16[1024,1024]{1,0:T(8,128)(2,1)}, u32[]{:S(2)}, u32[]{:S(2)}) collective-permute-start(bf16[1024,1024]{1,0:T(8,128)(2,1)} %bitcast.2), channel_id=1, source_target_pairs={{0,1},{1,0},{2,3},{3,2},{4,5},{5,4},{6,7},{7,6},{8,9},{9,8},{10,11... | collective-permute-start | bytes 6291464 | tf_op jit(solution)/shard_map/ppermute | solution.py:16
  194.5 29.2 %all-to-all-start = ((bf16[8,128,1024]{1,2,0:T(8,128)(2,1)}), bf16[8,128,1024]{1,2,0:T(8,128)(2,1)}, u32[]{:S(2)}, u32[]{:S(2)}) async-start(bf16[8,128,1024]{1,2,0:T(8,128)(2,1)} %bitcast.86), calls=%async_computation | async-start | bytes 4194304 | tf_op jit(solution)/shard_map/all_to_all | solution.py:89
  199.2 150.7 %all-gather.2.cloned.1.call-start = ((), (), s32[]{:S(2)}) async-start(), calls=%async_computation.3 | async-start | bytes 5242880 | tf_op jit(solution)/shard_map/all_gather | solution.py:120
  268.6 1.4 copy-start.3
  284.9 2.0 copy-start
Sparse Core Ops, SparseCore 0:
  23.2 156.1 all-reduce.2
  270.1 79.8 all-gather.1
where the time goes:
time: 395 us; the launch traced here: 392 us
  waiting for transfers between devices  233 us (59%)
  local copies, waits for them, and re-layouts  65.1 us (16%)
  blocking collectives  29.9 us (8%)
  other arithmetic  29.5 us (7%)
  between operations  16.3 us (4%)
  matrix products  13.8 us (3%)
  starting transfers between devices  4.87 us (1%)
    psum x1, waiting for transfers between devices, local(): lax.psum(replica_term.astype(jnp.bfloat16), 'rep').astype(jnp.float32)  155 us
    all_gather x1, waiting for transfers between devices, local(): everything = lax.all_gather(update_slab, 'rep', axis=1, tiled=True)  63 us
    unnamed x16, local copies, waits for them, and re-layouts  24.3 us
    all_to_all x1, blocking collectives, local(): lax.all_to_all(outgoing_rows, 'fsdp', split_axis=0, concat_axis=0, tiled=...  18.7 us
    all_to_all x1, waiting for transfers between devices, local(): lax.all_to_all(outgoing, 'fsdp', split_axis=0, concat_axis=0, tiled=True)  15.2 us
    select_n x2, other arithmetic, local(): jnp.take_along_axis(everything.reshape(band_count, sub_rows, columns, blo...  11.5 us
    gather x2, local copies, waits for them, and re-layouts, local(): jnp.take_along_axis(everything.reshape(band_count, sub_rows, columns, blo...  11.3 us
    psum x1, blocking collectives, local(): adam_total, product_total = lax.psum((adam_table, product_table), 'fsdp')  11.2 us
  transfers between devices with their start and end apart: 4, of which 3 were waited for; matrix products, arithmetic and copies ran while one was open for 11% of the time, Pallas kernels for 0%

commit v1 on v0

--- a/solution.py
+++ b/solution.py
@@ -1,6 +1,8 @@
 import jax
 import jax.numpy as jnp
 from jax import lax
+from jax.experimental import pallas as pl
+from jax.experimental.pallas import tpu as pltpu
 from jax.sharding import PartitionSpec as P
 
 NEWTON = 3
@@ -49,6 +51,55 @@
     return root_now
 
 
+def copy_block(order_ref, in_ref, out_ref):
+    out_ref[...] = in_ref[...].reshape(out_ref.shape)
+
+
+def owner_order(rows, col_order, groups, band_count, sub_rows, block_size):
+    per_group = col_order.shape[1] // groups
+    pairs = band_count * per_group
+
+    def source(i, order_ref):
+        group, pair = i // pairs, i % pairs
+        band, slot = pair // per_group, pair % per_group
+        return band, order_ref[band * groups * per_group + group * per_group + slot]
+
+    return pl.pallas_call(
+        copy_block,
+        grid_spec=pltpu.PrefetchScalarGridSpec(
+            num_scalar_prefetch=1,
+            grid=(groups * pairs,),
+            in_specs=[pl.BlockSpec((sub_rows, block_size), source)],
+            out_specs=pl.BlockSpec((1, sub_rows, block_size), lambda i, order_ref: (i, 0, 0)),
+        ),
+        out_shape=jax.ShapeDtypeStruct((groups * pairs, sub_rows, block_size), rows.dtype),
+        name="owner_order",
+    )(col_order.reshape(-1), rows)
+
+
+def natural_order(pieces, col_order, groups, band_count, sub_rows, block_size):
+    columns = col_order.shape[1]
+    per_group = columns // groups
+    pairs = band_count * per_group
+
+    def target(i, order_ref):
+        group, pair = i // pairs, i % pairs
+        band, slot = pair // per_group, pair % per_group
+        return band, order_ref[band * columns + group * per_group + slot]
+
+    return pl.pallas_call(
+        copy_block,
+        grid_spec=pltpu.PrefetchScalarGridSpec(
+            num_scalar_prefetch=1,
+            grid=(groups * pairs,),
+            in_specs=[pl.BlockSpec((1, sub_rows, block_size), lambda i, order_ref: (i, 0, 0))],
+            out_specs=pl.BlockSpec((sub_rows, block_size), target),
+        ),
+        out_shape=jax.ShapeDtypeStruct((band_count * sub_rows, columns * block_size), pieces.dtype),
+        name="natural_order",
+    )(col_order.reshape(-1), pieces)
+
+
 def local(grads, moments, factors, roots, refresh, owner):
     block_size = factors.shape[2]
     height = grads.shape[1]
@@ -69,20 +120,15 @@
     slot_index = local_index // 2
     col_range = jnp.arange(columns, dtype=jnp.int32)
     col_order = jnp.argsort(owner * columns + col_range[None, :], axis=1)
-    replica_term = grads[0].astype(jnp.float32)
-    summed = lax.psum(replica_term.astype(jnp.bfloat16), "rep").astype(jnp.float32)
-    mine_cols = lax.dynamic_slice_in_dim(col_order, group_index * per_group, per_group, 1)
-    owned_grad = jnp.take_along_axis(
-        summed.reshape(band_count, sub_rows, columns, block_size),
-        mine_cols[:, None, :, None],
-        axis=2,
-    )
-    gradient = owned_grad / groups
+    ordered = owner_order(grads[0], col_order, groups, band_count, sub_rows, block_size)
+    summed = lax.psum_scatter(ordered, "rep", scatter_dimension=0, tiled=True)
+    owned_grad = summed.reshape(band_count, per_group, sub_rows, block_size).astype(jnp.float32)
+    gradient = jnp.transpose(owned_grad, (0, 2, 1, 3)) / groups
     moment_old = moments.reshape(band_count, sub_rows, per_group, block_size)
     moment_new = BETA_MOMENT * moment_old + (1.0 - BETA_MOMENT) * gradient * gradient
     adam_dir = gradient / (jnp.sqrt(moment_new) + EPS_ADAM)
     adam_table = jnp.sum(adam_dir * adam_dir, axis=(1, 3))
-    pieces = jnp.transpose(gradient.astype(jnp.bfloat16), (0, 2, 1, 3)).reshape(
+    pieces = (owned_grad / groups).astype(jnp.bfloat16).reshape(
         band_count * per_group, sub_rows, block_size
     )
     outgoing = jnp.repeat(pieces, 2, axis=0)
@@ -114,16 +160,11 @@
     outgoing_rows = update_half.reshape(fsdp_count, sub_rows, half_cols)
     incoming_rows = lax.all_to_all(outgoing_rows, "fsdp", split_axis=0, concat_axis=0, tiled=True)
     arranged_rows = incoming_rows.reshape(band_count, per_group, 2, sub_rows, half_cols)
-    update_slab = jnp.transpose(arranged_rows, (0, 3, 1, 2, 4)).reshape(
-        height, per_group * block_size
-    )
-    everything = lax.all_gather(update_slab, "rep", axis=1, tiled=True)
-    inverse = jnp.argsort(col_order, axis=1)
-    update = jnp.take_along_axis(
-        everything.reshape(band_count, sub_rows, columns, block_size),
-        inverse[:, None, :, None],
-        axis=2,
-    ).reshape(height, width_all)
+    update_slab = jnp.transpose(arranged_rows, (0, 1, 3, 2, 4)).reshape(
+        band_count * per_group, sub_rows, block_size
+    )
+    everything = lax.all_gather(update_slab, "rep", axis=0, tiled=True)
+    update = natural_order(everything, col_order, groups, band_count, sub_rows, block_size)
     pair_ids = refresh // 2
     listed_band = pair_ids // columns
     listed_col = pair_ids % columns

time: 395 us -> 279 us (0.71)
  waiting for transfers between devices: 233 us -> 105 us
  matrix products: 13.8 us -> 54.3 us
  local copies, waits for them, and re-layouts: 65.1 us -> 28 us
  Pallas kernels: 0 us -> 21.6 us
  other arithmetic: 29.5 us -> 17 us
    psum x1 -> x0, waiting for transfers between devices: 155 us -> none  [local(): lax.psum(replica_term.astype(jnp.bfloat16), 'rep').astype(jnp.float32)]
    reduce_scatter x0 -> x1, waiting for transfers between devices: none -> 78 us  [local(): summed = lax.psum_scatter(ordered, 'rep', scatter_dimension=0, tiled=True)]
    all_gather x1, waiting for transfers between devices: 63 us -> 15.4 us  [local(): everything = lax.all_gather(update_slab, 'rep', axis=0, tiled=True)]
    dot_general x0 -> x5, matrix products: none -> 40.8 us  [the longest x2 20.1 us: newton_whole(): jnp.dot(square, square, preferred_element_type=jnp.float32)]
    pallas_call x0 -> x2, Pallas kernels: none -> 21.6 us  [the longest x1 10.8 us: natural_order(): pl.pallas_call(copy_block, grid_spec=pltpu.PrefetchScalarGridSpec(num_sca...]
    gather x4 -> x0, local copies, waits for them, and re-layouts: 17.2 us -> none  [the longest x2 11.3 us: local(): jnp.take_along_axis(everything.reshape(band_count, sub_rows, columns, blo...]
    unnamed x16, local copies, waits for them, and re-layouts: 24.3 us -> 11 us
    reshape x3 -> x1, local copies, waits for them, and re-layouts: 14.4 us -> 1.39 us  [local(): jnp.transpose(arranged_rows, (0, 1, 3, 2, 4))]
  transfers between devices with their start and end apart: 4 -> 4, of which waited for: 3 -> 3; matrix products, arithmetic and copies ran while one was open for 11% -> 29% of each run, Pallas kernels for 0% -> 0%
where the time goes in v1:
time: 279 us; the launch traced here: 277 us
  waiting for transfers between devices  105 us (38%)
  matrix products  54.3 us (19%)
  blocking collectives  29.8 us (11%)
  local copies, waits for them, and re-layouts  28 us (10%)
  Pallas kernels  21.6 us (8%)
  other arithmetic  17 us (6%)
  between operations  16.3 us (6%)
  starting transfers between devices  4.31 us (2%)
    reduce_scatter x1, waiting for transfers between devices, local(): summed = lax.psum_scatter(ordered, 'rep', scatter_dimension=0, tiled=True)  78 us
    dot_general x2, matrix products, newton_whole(): jnp.dot(square, square, preferred_element_type=jnp.float32)  20.1 us
    all_to_all x1, blocking collectives, local(): lax.all_to_all(outgoing_rows, 'fsdp', split_axis=0, concat_axis=0, tiled=...  18.7 us
    dot_general x2, matrix products, newton_whole(): jnp.dot(root_now, step_mat, preferred_element_type=jnp.float32)  15.5 us
    all_gather x1, waiting for transfers between devices, local(): everything = lax.all_gather(update_slab, 'rep', axis=0, tiled=True)  15.4 us
    all_to_all x1, waiting for transfers between devices, local(): lax.all_to_all(outgoing, 'fsdp', split_axis=0, concat_axis=0, tiled=True)  11.3 us
    psum x1, blocking collectives, local(): adam_total, product_total = lax.psum((adam_table, product_table), 'fsdp')  11.1 us
    unnamed x16, local copies, waits for them, and re-layouts  11 us
  transfers between devices with their start and end apart: 4, of which 3 were waited for; matrix products, arithmetic and copies ran while one was open for 29% of the time, Pallas kernels for 0%

profile of v1, /device:TPU:6, one launch (start us, length us, event | category | flops | bytes accessed | tf_op | source)
XLA Modules:
  0.0 276.7 jit_solution(4186757053340690105)
XLA Ops:
  7.2 3.1 %copy.61 = bf16[1,1,1024,1024]{3,2,1,0:T(8,128)(2,1)} copy(bf16[1,1,1024,1024]{3,2,1,0:T(8,128)(2,1)} %param.11) | data formatting | bytes 4194304
  11.8 10.8 %owner_order.1 = bf16[16,128,1024]{2,1,0:T(8,128)(2,1)} custom-call(s32[16]{0:T(128)} %reduce.1.order_ref, bf16[128,16384]{1,0:T(8,128)(2,1)} %bitcast.65), custom_call_target="tpu_custom_call" | custom-call | tf_op jit(solution)/shard_map/owner_order/pallas_call | solution.py:67
  22.7 78.0 %reduce-scatter.2.cloned.1.call-done = bf16[4,128,1024]{2,1,0:T(8,128)(2,1)} async-done(((bf16[16,128,1024]{2,1,0:T(8,128)(2,1)}), bf16[4,128,1024]{2,1,0:T(8,128)(2,1)}) %reduce-scatter.2.cloned.1.call-update) | async-done | bytes 1048592 | tf_op jit(solution)/shard_map/reduce_scatter | solution.py:124
  100.7 1.4 fusion.77
  102.8 1.6 broadcast_in_dim.33
  104.4 4.2 %all-to-all-start = ((bf16[8,128,1024]{1,2,0:T(8,128)(2,1)}), bf16[8,128,1024]{1,2,0:T(8,128)(2,1)S(1)}, u32[]{:S(2)}, u32[]{:S(2)}) async-start(bf16[8,128,1024]{1,2,0:T(8,128)(2,1)} %bitcast.59), calls=%async_computation.1 | async-start | bytes 4194304 | tf_op jit(solution)/shard_map/all_to_all | solution.py:135
  108.6 2.9 %copy.52 = f32[128,4096]{0,1:T(8,128)} copy(f32[128,4096]{1,0:T(8,128)} %param.9) | data formatting | bytes 4194304 | tf_op args[1]
  111.5 3.1 %broadcast_multiply_fusion = f32[128,4096]{0,1:T(8,128)} fusion(f32[128,4096]{0,1:T(8,128)} %copy.52), kind=kLoop, calls=%fused_computation.71 | loop fusion | flops 524288 | bytes 4194304 | tf_op jit(solution)/shard_map/mul | solution.py:128
  114.6 3.0 %copy.53 = f32[1,128,4,1024]{3,1,2,0:T(8,128)} copy(f32[1,128,4,1024]{1,3,2,0:T(8,128)} %bitcast.63) | data formatting | bytes 4194304 | tf_op jit(solution)/shard_map/mul | solution.py:128
  117.6 4.1 %fusion.80 = (f32[1,128,4,1024]{3,1,2,0:T(8,128)}, f32[4]{0:T(128)S(1)}) fusion(f32[1,128,4,1024]{3,1,2,0:T(8,128)} %copy.53, bf16[4,128,1024]{2,1,0:T(8,128)(2,1)S(1)} %copy-done.4), kind=kLoop, calls=%fused_computation.56 | loop fusion | flops 4718588 | bytes 5242896 | tf_op jit(solution)/shard_map/add | solution.py:128
  121.6 11.3 %all-to-all-done = bf16[8,128,1024]{1,2,0:T(8,128)(2,1)S(1)} async-done(((bf16[8,128,1024]{1,2,0:T(8,128)(2,1)}), bf16[8,128,1024]{1,2,0:T(8,128)(2,1)S(1)}, u32[]{:S(2)}, u32[]{:S(2)}) %all-to-all-start) | async-done | bytes 2097184 | tf_op jit(solution)/shard_map/all_to_all | solution.py:135
  132.9 2.6 copy.51
  135.5 7.1 %multiply_reduce_fusion.1 = (f32[]{:T(128)}, f32[1024,512]{1,0:T(8,128)S(1)}) fusion(bf16[1024,1024]{1,0:T(8,128)(2,1)} %bitcast.2, s32[]{:T(128)S(6)} %select_n.81, bf16[1024,1024]{1,0:T(8,128)(2,1)} %collective-permute-done, pred[]{:T(512)S(6)} %eq.62, bf16[1024,1024]{1,0:T(8,128)(2,1)} %bitcast.60), kind=kOutput, calls=%fused_computation.61 | convolution fusion | flops 3224895488 | bytes 10487300 | tf_op jit(solution)/shard_map/dot_general | solution.py:150
  143.3 11.1 %all-reduce = (f32[1,4]{1,0:T(1,128)S(1)}, f32[1,4]{1,0:T(1,128)S(1)}) all-reduce(f32[1,4]{1,0:T(1,128)S(1)} %bitcast.71, f32[1,4]{1,0:T(1,128)S(1)} %select_multiply_fusion), channel_id=1, replica_groups=mesh['rep'=4,'fsdp'=8] {'fsdp'}, use_global_device_ids=true, to_apply=%region_3.4 | all-reduce | flops 8 | bytes 64 | tf_op jit(solution)/shard_map/psum | solution.py:155
  156.8 18.7 %all_to_all.10 = bf16[8,128,512]{2,1,0:T(8,128)(2,1)S(1)} all-to-all(bf16[8,128,512]{2,1,0:T(8,128)(2,1)S(1)} %bitcast.66), channel_id=1, replica_groups=mesh['rep'=4,'fsdp'=8] {'fsdp'}, dimensions={0} | all-to-all | bytes 2097152 | tf_op jit(solution)/shard_map/all_to_all | solution.py:161
  176.2 1.4 copy.55
  179.9 1.8 copy.56
  181.7 3.0 %copy.58 = f32[128,4096]{1,0:T(8,128)} copy(f32[128,4096]{0,1:T(8,128)} %bitcast.64) | data formatting | bytes 4194304
  184.8 2.5 copy.57
  187.3 6.3 %bitcast_add_fusion = f32[1024,1024]{1,0:T(8,128)S(1)} fusion(f32[1,1,1024,1024]{3,2,1,0:T(8,128)} %param.10, bf16[1024,1024]{1,0:T(8,128)(2,1)S(1)} %bitcast.62, bf16[1024,1024]{0,1:T(8,128)(2,1)} %copy.57, pred[]{:T(512)S(6)} %eq.62), kind=kOutput, calls=%fused_computation.49 | convolution fusion | flops 2151677952 | bytes 12582913 | tf_op jit(solution)/shard_map/dot_general | solution.py:138
  193.6 2.0 copy-done
  195.6 48.1 %conditional.1 = (bf16[1,1,1024,1024]{3,2,1,0:T(8,128)(2,1)}) conditional(s32[]{:T(128)} %convert_element_type.85, bf16[1024,1024]{1,0:T(8,128)(2,1)} %bitcast.2, f32[1024,1024]{1,0:T(8,128)S(1)} %bitcast_add_fusion), branch_computations={%region_10.11_spmd, %region_11.13_spmd} | conditional | flops 19371393024 | bytes 65011804 | solution.py:181
  195.6 2.0 copy-done.1
  197.7 1.7 multiply_reduce_fusion
  200.1 2.8 %divide_convert_fusion = bf16[1024,1024]{1,0:T(8,128)(2,1)S(1)} fusion(f32[1024,1024]{1,0:T(8,128)} %copy-done.1, f32[]{:T(128)S(6)} %sqrt.6), kind=kLoop, calls=%fused_computation.10 | loop fusion | flops 2097152 | bytes 6291460 | tf_op jit(solution)/shard_map/cond/branch_1_fun/convert_element_type | solution.py:23
  202.8 8.0 %fusion.17 = bf16[1024,1024]{1,0:T(8,128)(2,1)} fusion(bf16[1024,1024]{1,0:T(8,128)(2,1)S(1)} %divide_convert_fusion), kind=kOutput, calls=%fused_computation.25 | convolution fusion | flops 4302307328 | bytes 4194304 | tf_op jit(solution)/shard_map/cond/branch_1_fun/dot_general | solution.py:45
  210.9 5.3 %fusion.26 = bf16[1024,1024]{1,0:T(8,128)(2,1)} fusion(bf16[1024,1024]{1,0:T(8,128)(2,1)S(1)} %divide_convert_fusion, bf16[1024,1024]{1,0:T(8,128)(2,1)} %fusion.17), kind=kOutput, calls=%fused_computation.34 | convolution fusion | flops 2148532224 | bytes 6291456 | tf_op jit(solution)/shard_map/cond/branch_1_fun/dot_general | solution.py:48
  216.1 7.5 %fusion.19 = bf16[1024,1024]{1,0:T(8,128)(2,1)} fusion(bf16[1024,1024]{1,0:T(8,128)(2,1)} %fusion.26, bf16[]{:T(256)S(6)} %pow.2, bf16[1024,1024]{1,0:T(8,128)(2,1)S(1)} %divide_convert_fusion), kind=kOutput, calls=%fused_computation.27 | convolution fusion | flops 4310695936 | bytes 6291458 | tf_op jit(solution)/shard_map/cond/branch_1_fun/dot_general | solution.py:38
  223.6 12.0 %fusion.12 = bf16[1024,1024]{1,0:T(8,128)(2,1)} fusion(bf16[1024,1024]{1,0:T(8,128)(2,1)} %fusion.26), kind=kOutput, calls=%fused_computation.20 | convolution fusion | flops 4302307328 | bytes 4194304 | tf_op jit(solution)/shard_map/cond/branch_1_fun/dot_general | solution.py:45
  235.6 8.0 %convert_bitcast_fusion = bf16[1,1,1024,1024]{3,2,1,0:T(8,128)(2,1)} fusion(bf16[1024,1024]{1,0:T(8,128)(2,1)} %fusion.19, bf16[1024,1024]{1,0:T(8,128)(2,1)S(1)} %copy-done.7, bf16[1024,1024]{1,0:T(8,128)(2,1)} %fusion.12), kind=kOutput, calls=%fused_computation.16 | convolution fusion | flops 4303355904 | bytes 8388608 | tf_op jit(solution)/shard_map/cond/branch_1_fun/dot_general | solution.py:38
  243.7 15.4 %all-gather.2.cloned.1.call-done.in_ref = bf16[16,128,1024]{2,1,0:T(8,128)(2,1)} async-done(((bf16[4,128,1024]{2,1,0:T(8,128)(2,1)}), bf16[16,128,1024]{2,1,0:T(8,128)(2,1)}) %all-gather.2.cloned.1.call-update) | async-done | bytes 4194320 | tf_op jit(solution)/shard_map/all_gather | solution.py:166
  259.1 10.8 %natural_order.1 = bf16[128,16384]{1,0:T(8,128)(2,1)} custom-call(s32[16]{0:T(128)} %reduce.1.order_ref, bf16[16,128,1024]{2,1,0:T(8,128)(2,1)} %all-gather.2.cloned.1.call-done.in_ref), custom_call_target="tpu_custom_call" | custom-call | tf_op jit(solution)/shard_map/natural_order/pallas_call | solution.py:90
  (40 shorter events, 6.2 us)
Async XLA Ops:
  7.2 3.1 %copy-start.5 = (s32[1,16]{1,0:T(1,128)S(1)}, s32[1,16]{1,0:T(1,128)}, u32[]{:S(2)}) copy-start(s32[1,16]{1,0:T(1,128)} %param.13) | copy-start | bytes 196
  7.2 93.5 %reduce-scatter.2.cloned.1.call-start = ((), (), s32[]{:S(2)}) async-start(), calls=%async_computation.3 | async-start | bytes 5242880 | tf_op jit(solution)/shard_map/reduce_scatter | solution.py:124
  22.6 112.9 %collective-permute-start = (bf16[1024,1024]{1,0:T(8,128)(2,1)}, bf16[1024,1024]{1,0:T(8,128)(2,1)}, u32[]{:S(2)}, u32[]{:S(2)}) collective-permute-start(bf16[1024,1024]{1,0:T(8,128)(2,1)} %bitcast.2), channel_id=1, source_target_pairs={{0,1},{1,0},{2,3},{3,2},{4,5},{5,4},{6,7},{7,6},{8,9},{9,8},{10,11... | collective-permute-start | bytes 6291464 | tf_op jit(solution)/shard_map/ppermute | solution.py:18
  104.4 28.5 %all-to-all-start = ((bf16[8,128,1024]{1,2,0:T(8,128)(2,1)}), bf16[8,128,1024]{1,2,0:T(8,128)(2,1)S(1)}, u32[]{:S(2)}, u32[]{:S(2)}) async-start(bf16[8,128,1024]{1,2,0:T(8,128)(2,1)} %bitcast.59), calls=%async_computation.1 | async-start | bytes 4194304 | tf_op jit(solution)/shard_map/all_to_all | solution.py:135
  108.6 150.4 %all-gather.2.cloned.1.call-start = ((), (), s32[]{:S(2)}) async-start(), calls=%async_computation.4 | async-start | bytes 5242880 | tf_op jit(solution)/shard_map/all_gather | solution.py:166
  114.6 3.0 %copy-start.4 = (bf16[4,128,1024]{2,1,0:T(8,128)(2,1)S(1)}, bf16[4,128,1024]{2,1,0:T(8,128)(2,1)}, u32[]{:S(2)}) copy-start(bf16[4,128,1024]{2,1,0:T(8,128)(2,1)} %reduce-scatter.2.cloned.1.call-done) | copy-start | bytes 3145732
  176.2 1.4 copy-start.6
  176.2 3.7 %copy-start.2 = (f32[1,128,4,1024]{3,1,2,0:T(8,128)S(1)}, f32[1,128,4,1024]{3,1,2,0:T(8,128)}, u32[]{:S(2)}) copy-start(f32[1,128,4,1024]{3,1,2,0:T(8,128)} %get-tuple-element.45) | copy-start | bytes 6291460
  181.7 3.0 %copy-start.3 = (bf16[8,128,1024]{2,1,0:T(8,128)(2,1)S(1)}, bf16[8,128,1024]{2,1,0:T(8,128)(2,1)}, u32[]{:S(2)}) copy-start(bf16[8,128,1024]{2,1,0:T(8,128)(2,1)} %copy.51) | copy-start | bytes 6291460
  193.6 2.0 copy-start
  195.6 2.0 copy-start.1
  223.6 12.0 %copy-start.7 = (bf16[1024,1024]{1,0:T(8,128)(2,1)S(1)}, bf16[1024,1024]{1,0:T(8,128)(2,1)}, u32[]{:S(2)}) copy-start(bf16[1024,1024]{1,0:T(8,128)(2,1)} %fusion.26) | copy-start | bytes 6291460 | tf_op jit(solution)/shard_map/cond
Sparse Core Ops, SparseCore 0:
  22.7 77.9 reduce-scatter.1
  177.7 81.2 all-gather.1
